TPU v7x, 32 devices: a whole 2x2x4 slice. The times are simulated.
32 devices in a mesh: face: 4 (over y, x), tile: 8 (over z, core).
Axes of the slice: x: 2, y: 2, z: 4, core: 2. Of those that a mesh axis runs over, the one named last changes fastest.
Arguments:
- state_field: bfloat16 [4, 256, 512, 256], P(None, 'face', 'tile'), may hold values from -6 to 6
- cotangent: bfloat16 [4, 256, 512, 256], P(None, 'face', 'tile'), may hold values from -6 to 6
- depth_weight: float32 [9, 256], replicated, may hold values from -2 to 2
- depth_bias: float32 [256], replicated, may hold values from -3 to 3
- point_weight: bfloat16 [256, 256], replicated, may hold values from -0.375 to 0.375
- tile_links: int32 [32, 4], P(('face', 'tile')), may hold values from 0 to 31, as said below
- link_sides: int32 [32, 4], P(('face', 'tile')), may hold values from 0 to 3
- link_flips: int32 [32, 4], P(('face', 'tile')), may hold values from 0 to 1
- corner_masks: int32 [32, 4], P(('face', 'tile')), may hold values 0 or 1
Outputs:
- field_grad: bfloat16 [4, 256, 512, 256], P(None, 'face', 'tile')
- depth_grad: float32 [9, 256], replicated
- bias_grad: float32 [256], replicated
- point_grad: float32 [256, 256], replicated
Inputs may be any that keep to these rules, and one draw needn't show every extreme that they name: Tile ids number the grid row by row, the row being the index along face. The four neighbours of a tile are the four tiles one step away along face or along tile with wrap-around, each exactly once. Links are mutual: if tile_links[a, s] = b and link_sides[a, s] = o then tile_links[b, o] = a, link_sides[b, o] = s and link_flips[b, o] = link_flips[a, s].
All inputs are finite; a program needn't handle non-finite values. No bound on the sum of `corner_masks` on one device may be relied on, other than what follows from the above.
Results may differ from a plain program's by a relative error of at most 0.0049.
Values may be sent and summed in bfloat16 or wider, within the bound.
A program may use at most 192 MiB of HBM per device.

v0:
```python
import functools

import jax
import jax.numpy as jnp
from jax import lax
from jax.experimental import pallas as pl
from jax.experimental.pallas import tpu as pltpu
from jax.sharding import PartitionSpec as P

root_two_pi = 0.7978845608028654
cubic_coef = 0.044715
HALF = 128
STRIP = 16
ROWS = 16
F32 = jnp.float32
BF16 = jnp.bfloat16


def gelu_pair(hidden):
    square = hidden * hidden
    gate = 0.5 + 0.5 * jnp.tanh(hidden * (root_two_pi + (root_two_pi * cubic_coef) * square))
    output = hidden * gate
    slope = gate + output * (1.0 - gate) * (
        2.0 * root_two_pi + (6.0 * root_two_pi * cubic_coef) * square
    )
    return output, slope


def first_kernel(
    norm_scale,
    x_ref,
    cot_ref,
    ends_ref,
    west_ref,
    east_ref,
    taps_ref,
    bias_ref,
    point_ref,
    g_ref,
    gnorth_ref,
    gsouth_ref,
    gwest_ref,
    geast_ref,
    sums_ref,
    win,
    grad_act,
    act,
    parts,
):
    sample, step = pl.program_id(0), pl.program_id(1)
    side, channels = x_ref.shape[1], x_ref.shape[3]
    rows = cot_ref.shape[1]

    @pl.when(step == 0)
    def _():
        for col_off in range(3):
            win[col_off, 0] = ends_ref[0, 0, col_off].astype(F32)
            win[col_off, side + 1] = ends_ref[0, 1, col_off].astype(F32)
        spot = lax.broadcasted_iota(jnp.int32, (side, HALF), 0)
        for lane in range(0, channels, HALF):
            lanes = pl.ds(lane, HALF)

            def shift(i, carry):
                mid = x_ref[0, i, :, lanes].astype(F32)
                win[1, i + 1, :, lanes] = mid
                win[0, i + 1, :, lanes] = jnp.where(
                    spot == 0, west_ref[0, i, :, lanes], pltpu.roll(mid, 1, 0)
                )
                win[2, i + 1, :, lanes] = jnp.where(
                    spot == side - 1, east_ref[0, i, :, lanes], pltpu.roll(mid, side - 1, 0)
                )
                return carry

            lax.fori_loop(0, side, shift, 0, unroll=2)

    @pl.when((step == 0) & (sample == 0))
    def _():
        sums_ref[...] = jnp.zeros_like(sums_ref)
        parts[...] = jnp.zeros_like(parts)

    cot = cot_ref[0].reshape(rows * side, channels)
    grad_act[...] = lax.dot_general(
        cot, point_ref[...], (((1,), (1,)), ((), ())), preferred_element_type=F32
    ).reshape(rows, side, channels)
    for lane in range(0, channels, HALF):
        lanes = pl.ds(lane, HALF)

        def row(k, held):
            held = list(held)
            i = step * rows + k
            for low in range(0, side, STRIP):
                spots = pl.ds(low, STRIP)
                views = [
                    win[col_off, i + row_off, spots, lanes]
                    for row_off in range(3)
                    for col_off in range(3)
                ]
                hidden = bias_ref[0:1, lanes] + taps_ref[0:1, lanes] * views[0]
                for t in range(1, 9):
                    hidden = hidden + taps_ref[t : t + 1, lanes] * views[t]
                output, slope = gelu_pair(hidden)
                act[k, spots, lanes] = output.astype(BF16)
                grad = (grad_act[k, spots, lanes] * slope).astype(BF16)
                g_ref[0, k, spots, lanes] = grad
                grad = grad.astype(F32)
                if low == 0:
                    gwest_ref[0, i, :, lanes] = grad[:1]
                if low + STRIP == side:
                    geast_ref[0, i, :, lanes] = grad[STRIP - 1 :]
                for t in range(9):
                    term = grad * views[t]
                    held[t] = held[t] + (term[:8] + term[8:])
                held[9] = held[9] + (grad[:8] + grad[8:])
            return tuple(held)

        held = lax.fori_loop(0, rows, row, tuple(parts[t, :, lanes] for t in range(10)))
        for t in range(10):
            parts[t, :, lanes] = held[t]
    sums_ref[0:channels] += lax.dot_general(
        act[...].reshape(rows * side, channels),
        cot,
        (((0,), (0,)), ((), ())),
        preferred_element_type=F32,
    )

    @pl.when(step == 0)
    def _():
        gnorth_ref[0] = g_ref[0, 0].astype(F32)

    @pl.when(step == pl.num_programs(1) - 1)
    def _():
        gsouth_ref[0] = g_ref[0, rows - 1].astype(F32)

    @pl.when((step == pl.num_programs(1) - 1) & (sample == pl.num_programs(0) - 1))
    def _():
        for t in range(10):
            sums_ref[channels + t : channels + t + 1] = jnp.sum(parts[t], axis=0, keepdims=True)
        sums_ref[...] = sums_ref[...] * norm_scale


def second_kernel(g_ref, north_ref, south_ref, west_ref, east_ref, taps_ref, out_ref):
    side, channels = g_ref.shape[1], g_ref.shape[3]
    spot = lax.broadcasted_iota(jnp.int32, (side, HALF), 0)
    for lane in range(0, channels, HALF):
        lanes = pl.ds(lane, HALF)

        def mixed(i, before, here, after):
            cols = [
                taps_ref[c : c + 1, lanes] * after
                + taps_ref[3 + c : 4 + c, lanes] * here
                + taps_ref[6 + c : 7 + c, lanes] * before
                for c in range(3)
            ]
            from_right = jnp.where(
                spot == side - 1, east_ref[0, i, :, lanes], pltpu.roll(cols[0], side - 1, 0)
            )
            from_left = jnp.where(
                spot == 0, west_ref[0, i, :, lanes], pltpu.roll(cols[2], 1, 0)
            )
            return cols[1] + from_right + from_left

        def load(i):
            return g_ref[0, i, :, lanes].astype(F32)

        empty = jnp.zeros((side, HALF), F32)
        first, second = load(0), load(1)
        out_ref[0, 0, :, lanes] = (
            mixed(0, empty, first, second) + north_ref[0, :, lanes].astype(F32)
        ).astype(BF16)

        def row(i, held):
            after = load(i + 1)
            out_ref[0, i, :, lanes] = mixed(i, held[0], held[1], after).astype(BF16)
            return held[1], after

        before, here = lax.fori_loop(1, side - 1, row, (first, second))
        out_ref[0, side - 1, :, lanes] = (
            mixed(side - 1, before, here, empty) + south_ref[0, :, lanes].astype(F32)
        ).astype(BF16)


def exchange(by_dir):
    face_count, tile_count = lax.axis_size("face"), lax.axis_size("tile")
    up = [(i, (i + 1) % face_count) for i in range(face_count)]
    right = [(i, (i + 1) % tile_count) for i in range(tile_count)]
    down = [(b, a) for a, b in up]
    left = [(b, a) for a, b in right]
    return jnp.stack(
        [
            lax.ppermute(by_dir[2], "face", up),
            lax.ppermute(by_dir[3], "tile", left),
            lax.ppermute(by_dir[0], "face", down),
            lax.ppermute(by_dir[1], "tile", right),
        ]
    )


def comm_kernel(
    face_count,
    tile_count,
    leaving_ref,
    sums_ref,
    returned_ref,
    point_ref,
    depth_ref,
    bias_ref,
    rims,
    face_box,
    face_extra,
    tile_box,
    tile_extra,
    part,
    extra,
    total,
    rim_send,
    rim_recv,
    face_send,
    face_recv,
    face_xsend,
    face_xrecv,
    tile_send,
    tile_recv,
    tile_xsend,
    tile_xrecv,
    tile_gsend,
    tile_grecv,
    face_gsend,
    face_grecv,
):
    face, tile = lax.axis_index("face"), lax.axis_index("tile")
    channels = point_ref.shape[0]
    block = channels // face_count
    owners = min(tile_count, block // 8)
    piece = block // owners

    def copy(src, dst, send_sem, recv_sem, to_face, to_tile):
        return pltpu.make_async_remote_copy(
            src_ref=src,
            dst_ref=dst,
            send_sem=send_sem,
            recv_sem=recv_sem,
            device_id=(to_face, to_tile),
            device_id_type=pl.DeviceIdType.MESH,
        )

    faces = [
        (k, lax.rem(face + k, face_count), lax.rem(face + face_count - k, face_count))
        for k in range(1, face_count)
    ]
    tiles = [
        (k, lax.rem(tile + k, tile_count), lax.rem(tile + tile_count - k, tile_count))
        for k in range(1, tile_count)
    ]

    barrier = pltpu.get_barrier_semaphore()
    for _, to, _ in faces:
        pl.semaphore_signal(
            barrier, inc=1, device_id=(to, tile), device_id_type=pl.DeviceIdType.MESH
        )
    for _, to, _ in tiles:
        pl.semaphore_signal(
            barrier, inc=1, device_id=(face, to), device_id_type=pl.DeviceIdType.MESH
        )
    pl.semaphore_wait(barrier, face_count + tile_count - 2)

    def rows_of(index, size):
        return pl.ds(pl.multiple_of(index * size, 8), size)

    sent = []
    for k, to, _ in faces:
        sent.append(
            copy(
                sums_ref.at[rows_of(to, block)],
                face_box.at[face],
                face_send.at[k],
                face_recv.at[face],
                to,
                tile,
            )
        )
        sent.append(
            copy(
                sums_ref.at[pl.ds(channels, 16)],
                face_extra.at[face],
                face_xsend.at[k],
                face_xrecv.at[face],
                to,
                tile,
            )
        )
    up, down = lax.rem(face + face_count - 1, face_count), lax.rem(face + 1, face_count)
    left, right = lax.rem(tile + tile_count - 1, tile_count), lax.rem(tile + 1, tile_count)
    rim_copies = [
        copy(leaving_ref.at[d], rims.at[(d + 2) % 4], rim_send.at[d], rim_recv.at[(d + 2) % 4], *to)
        for d, to in enumerate([(up, tile), (face, right), (down, tile), (face, left)])
    ]
    for one in sent + rim_copies:
        one.start()
    face_box[face] = sums_ref[rows_of(face, block)]
    face_extra[face] = sums_ref[channels : channels + 16]
    for k, to, source in faces:
        copy(
            face_box.at[source], face_box.at[source], face_send.at[k], face_recv.at[source], to, tile
        ).wait_recv()
        copy(
            face_extra.at[source],
            face_extra.at[source],
            face_xsend.at[k],
            face_xrecv.at[source],
            to,
            tile,
        ).wait_recv()
    acc, small = face_box[0], face_extra[0]
    for f in range(1, face_count):
        acc, small = acc + face_box[f], small + face_extra[f]
    part[...] = acc
    extra[...] = small

    for k, to, _ in tiles:

        @pl.when(to < owners)
        def _():
            copy(
                part.at[rows_of(to, piece)],
                tile_box.at[tile],
                tile_send.at[k],
                tile_recv.at[tile],
                face,
                to,
            ).start()

        one = copy(
            extra, tile_extra.at[tile], tile_xsend.at[k], tile_xrecv.at[tile], face, to
        )
        one.start()
        sent.append(one)
    tile_extra[tile] = extra[...]

    @pl.when(tile < owners)
    def _():
        tile_box[tile] = part[rows_of(tile, piece)]
        for k, to, source in tiles:
            copy(
                tile_box.at[source],
                tile_box.at[source],
                tile_send.at[k],
                tile_recv.at[source],
                face,
                to,
            ).wait_recv()
        acc = tile_box[0]
        for t in range(1, tile_count):
            acc = acc + tile_box[t]
        mine = rows_of(face * owners + tile, piece)
        total[mine] = acc
        for k, to, _ in tiles:
            copy(
                total.at[mine], total.at[mine], tile_gsend.at[k], tile_grecv.at[tile], face, to
            ).start()

    for k, to, source in tiles:

        @pl.when(source < owners)
        def _():
            theirs = rows_of(face * owners + source, piece)
            copy(
                total.at[theirs], total.at[theirs], tile_gsend.at[k], tile_grecv.at[source], face, to
            ).wait_recv()

    mine = rows_of(face, block)
    for k, to, _ in faces:
        one = copy(total.at[mine], total.at[mine], face_gsend.at[k], face_grecv.at[face], to, tile)
        one.start()
        sent.append(one)
    for k, to, source in tiles:
        copy(
            tile_extra.at[source],
            tile_extra.at[source],
            tile_xsend.at[k],
            tile_xrecv.at[source],
            face,
            to,
        ).wait_recv()
    small = tile_extra[0]
    for t in range(1, tile_count):
        small = small + tile_extra[t]
    depth_ref[...] = small[:9]
    bias_ref[...] = small[9:10]
    for one in rim_copies:
        one.wait_recv()
    returned_ref[...] = rims[...]
    for k, to, source in faces:
        theirs = rows_of(source, block)
        copy(
            total.at[theirs], total.at[theirs], face_gsend.at[k], face_grecv.at[source], to, tile
        ).wait_recv()
    point_ref[...] = total[...]
    for one in sent + rim_copies:
        one.wait_send()
    for k, to, _ in tiles:

        @pl.when(to < owners)
        def _():
            copy(
                part.at[rows_of(to, piece)],
                tile_box.at[tile],
                tile_send.at[k],
                tile_recv.at[tile],
                face,
                to,
            ).wait_send()

        @pl.when(tile < owners)
        def _():
            own = rows_of(face * owners + tile, piece)
            copy(
                total.at[own], total.at[own], tile_gsend.at[k], tile_grecv.at[tile], face, to
            ).wait_send()


def return_and_sum(leaving, sums):
    face_count, tile_count = lax.axis_size("face"), lax.axis_size("tile")
    channels = sums.shape[1]
    block = channels // face_count
    piece = block // min(tile_count, block // 8)
    vmem = pl.BlockSpec(memory_space=pltpu.VMEM)
    dma = pltpu.SemaphoreType.DMA
    return pl.pallas_call(
        functools.partial(comm_kernel, face_count, tile_count),
        in_specs=[vmem, vmem],
        out_specs=[vmem] * 4,
        out_shape=[
            jax.ShapeDtypeStruct(leaving.shape, BF16),
            jax.ShapeDtypeStruct((channels, channels), F32),
            jax.ShapeDtypeStruct((9, channels), F32),
            jax.ShapeDtypeStruct((1, channels), F32),
        ],
        scratch_shapes=[
            pltpu.VMEM(leaving.shape, BF16),
            pltpu.VMEM((face_count, block, channels), F32),
            pltpu.VMEM((face_count, 16, channels), F32),
            pltpu.VMEM((tile_count, piece, channels), F32),
            pltpu.VMEM((tile_count, 16, channels), F32),
            pltpu.VMEM((block, channels), F32),
            pltpu.VMEM((16, channels), F32),
            pltpu.VMEM((channels, channels), F32),
            dma((4,)),
            dma((4,)),
        ]
        + [dma((face_count,))] * 4
        + [dma((tile_count,))] * 6
        + [dma((face_count,))] * 2,
        compiler_params=pltpu.CompilerParams(
            collective_id=0, has_side_effects=True, vmem_limit_bytes=32 * 2**20
        ),
    )(leaving, sums)


def window_rows(first, row, last):
    row = jnp.concatenate([first[:, None], row, last[:, None]], axis=1)
    side = row.shape[1] - 2
    return jnp.stack([row[:, c : c + side] for c in range(3)], axis=1)


def end_windows(rim_rows, cmask):
    rim32 = rim_rows.astype(F32)
    north_west = (cmask[0] * 0.5 * (rim32[0][:, 0] + rim32[3][:, 0])).astype(BF16)
    north_east = (cmask[1] * 0.5 * (rim32[0][:, -1] + rim32[1][:, 0])).astype(BF16)
    south_east = (cmask[2] * 0.5 * (rim32[1][:, -1] + rim32[2][:, -1])).astype(BF16)
    south_west = (cmask[3] * 0.5 * (rim32[2][:, 0] + rim32[3][:, -1])).astype(BF16)
    return jnp.stack(
        [
            window_rows(north_west, rim_rows[0], north_east),
            window_rows(south_west, rim_rows[2], south_east),
        ],
        axis=1,
    )


def rim_terms(tap_rows, edges, mask_low, mask_high):
    length = edges.shape[2]
    spot = lax.broadcasted_iota(jnp.int32, (1, 1, length, 1), 2)
    padded_rows = jnp.pad(edges, ((0, 0), (0, 0), (1, 1), (0, 0)))
    tap_first = tap_rows[:, 0][:, None, None, :]
    tap_middle = tap_rows[:, 1][:, None, None, :]
    tap_last = tap_rows[:, 2][:, None, None, :]
    return (
        (tap_first * padded_rows[:, :, 2:] + tap_middle * edges)
        + tap_last * padded_rows[:, :, :-2]
        + jnp.where(spot == 0, (0.5 * mask_low) * tap_first * edges, 0.0)
        + jnp.where(spot == length - 1, (0.5 * mask_high) * tap_last * edges, 0.0)
    )


def shards(
    state_field,
    cotangent,
    depth_weight,
    depth_bias,
    point_weight,
    tile_links,
    link_sides,
    link_flips,
    corner_masks,
):
    batch, side, _, channels = state_field.shape
    face_count = lax.axis_size("face")
    tile_count = lax.axis_size("tile")
    face_pos = lax.axis_index("face")
    tile_pos = lax.axis_index("tile")
    toward = jnp.stack(
        [
            (face_pos - 1) % face_count * tile_count + tile_pos,
            face_pos * tile_count + (tile_pos + 1) % tile_count,
            (face_pos + 1) % face_count * tile_count + tile_pos,
            face_pos * tile_count + (tile_pos - 1) % tile_count,
        ]
    )
    matched = tile_links[0][:, None] == toward[None, :]
    counter = jnp.arange(4, dtype=jnp.int32)
    dir_of_side = jnp.sum(jnp.where(matched, counter[None, :], 0), axis=1)
    side_of_dir = jnp.sum(jnp.where(matched, counter[:, None], 0), axis=0)
    flip_side = (link_flips[0] == 1)[:, None, None, None]
    cmask = corner_masks[0].astype(F32)
    norm_scale = float(batch * side * side * face_count * tile_count) ** (-0.5)

    def toward_sides(by_dir):
        got = jnp.take(by_dir, dir_of_side, axis=0)
        return jnp.where(flip_side, got[:, :, ::-1], got)

    edges = jnp.stack(
        [state_field[:, 0], state_field[:, :, -1], state_field[:, -1], state_field[:, :, 0]]
    )
    rim_rows = toward_sides(exchange(jnp.take(edges, side_of_dir, axis=0)))
    ends = end_windows(rim_rows, cmask)

    whole = pl.BlockSpec((1, side, side, channels), lambda b, s: (b, 0, 0, 0))
    rows_of = pl.BlockSpec((1, ROWS, side, channels), lambda b, s: (b, s, 0, 0))
    line = pl.BlockSpec((1, side, 1, channels), lambda b, s: (b, 0, 0, 0))
    flat = pl.BlockSpec((1, side, channels), lambda b, s: (b, 0, 0))
    fixed = lambda *shape: pl.BlockSpec(shape, lambda b, s: (0,) * len(shape))
    pixels = batch * side * side
    sum_rows = channels + 16
    grad_hidden, grad_north, grad_south, grad_west, grad_east, sums = pl.pallas_call(
        functools.partial(first_kernel, norm_scale),
        grid=(batch, side // ROWS),
        in_specs=[
            whole,
            rows_of,
            pl.BlockSpec((1, 2, 3, side, channels), lambda b, s: (b, 0, 0, 0, 0)),
            line,
            line,
            fixed(9, channels),
            fixed(1, channels),
            fixed(channels, channels),
        ],
        out_specs=[rows_of, flat, flat, line, line, fixed(sum_rows, channels)],
        out_shape=[
            jax.ShapeDtypeStruct(state_field.shape, BF16),
            jax.ShapeDtypeStruct((batch, side, channels), F32),
            jax.ShapeDtypeStruct((batch, side, channels), F32),
            jax.ShapeDtypeStruct((batch, side, 1, channels), F32),
            jax.ShapeDtypeStruct((batch, side, 1, channels), F32),
            jax.ShapeDtypeStruct((sum_rows, channels), F32),
        ],
        scratch_shapes=[
            pltpu.VMEM((3, side + 2, side, channels), F32),
            pltpu.VMEM((ROWS, side, channels), F32),
            pltpu.VMEM((ROWS, side, channels), BF16),
            pltpu.VMEM((10, 8, channels), F32),
        ],
        compiler_params=pltpu.CompilerParams(vmem_limit_bytes=48 * 2**20),
        cost_estimate=pl.CostEstimate(
            flops=4 * pixels * channels * channels,
            bytes_accessed=6 * pixels * channels,
            transcendentals=pixels * channels,
        ),
    )(
        state_field,
        cotangent,
        ends,
        rim_rows[3].astype(F32)[:, :, None],
        rim_rows[1].astype(F32)[:, :, None],
        depth_weight,
        depth_bias[None],
        point_weight,
    )

    tap_table = depth_weight.reshape(3, 3, channels)
    side_taps = jnp.stack([tap_table[0], tap_table[:, 2], tap_table[2], tap_table[:, 0]], axis=0)
    mask_low = cmask[jnp.array([0, 1, 3, 0])][:, None, None, None]
    mask_high = cmask[jnp.array([1, 2, 2, 3])][:, None, None, None]
    grad_edges = jnp.stack(
        [
            grad_north,
            grad_east[:, :, 0],
            grad_south,
            grad_west[:, :, 0],
        ]
    )
    leaving = rim_terms(side_taps, grad_edges, mask_low, mask_high).astype(BF16)
    leaving = jnp.take(leaving, side_of_dir, axis=0)
    returned, point_sum, depth_sum, bias_sum = return_and_sum(
        leaving.reshape(4, batch * side, channels), sums
    )
    incoming = toward_sides(returned.reshape(leaving.shape))

    whole = pl.BlockSpec((1, side, side, channels), lambda b: (b, 0, 0, 0))
    line = pl.BlockSpec((1, side, 1, channels), lambda b: (b, 0, 0, 0))
    flat = pl.BlockSpec((1, side, channels), lambda b: (b, 0, 0))
    field_grad = pl.pallas_call(
        second_kernel,
        grid=(batch,),
        in_specs=[whole, flat, flat, line, line, pl.BlockSpec((9, channels), lambda b: (0, 0))],
        out_specs=whole,
        out_shape=jax.ShapeDtypeStruct(state_field.shape, BF16),
        compiler_params=pltpu.CompilerParams(vmem_limit_bytes=48 * 2**20),
        cost_estimate=pl.CostEstimate(
            flops=40 * pixels * channels,
            bytes_accessed=4 * pixels * channels,
            transcendentals=0,
        ),
    )(
        grad_hidden,
        incoming[0],
        incoming[2],
        incoming[3].astype(F32)[:, :, None],
        incoming[1].astype(F32)[:, :, None],
        depth_weight,
    )
    return field_grad, depth_sum, bias_sum[0], point_sum


def solution(mesh):
    in_specs = (
        P(None, "face", "tile", None),
        P(None, "face", "tile", None),
        P(),
        P(),
        P(),
        P(("face", "tile"), None),
        P(("face", "tile"), None),
        P(("face", "tile"), None),
        P(("face", "tile"), None),
    )
    out_specs = (P(None, "face", "tile", None), P(), P(), P())
    return jax.shard_map(shards, mesh=mesh, in_specs=in_specs, out_specs=out_specs, check_vma=False)
```

profile of v0, /device:TPU:0, one launch (start us, length us, event | category | flops | bytes accessed | tf_op | source)
XLA Modules:
  0.0 136.7 jit_solution(3716062163192810226)
XLA Ops:
  0.7 1.0 slice_bitcast_fusion.13
  1.7 2.0 %fusion.18 = (bf16[4,64,1,256]{3,2,1,0:T(2,128)(2,1)S(1)}, bf16[4,64,1,256]{3,2,1,0:T(2,128)(2,1)S(1)}) fusion(bf16[4,64,64,256]{3,2,1,0:T(8,128)(2,1)} %x_ref.1), kind=kLoop, calls=%fused_computation.99 | loop fusion | bytes 524288 | tf_op jit(solution)/shard_map/slice | solution.py:532
  3.8 0.8 fusion.17
  4.8 0.6 gather_fusion.2
  5.5 3.0 %collective-permute-start = (bf16[4,64,256]{2,1,0:T(8,128)(2,1)S(1)}, bf16[4,64,256]{2,1,0:T(8,128)(2,1)S(1)}, u32[]{:S(2)}, u32[]{:S(2)}) collective-permute-start(bf16[4,64,256]{2,1,0:T(8,128)(2,1)S(1)} %get-tuple-element.46), channel_id=1, source_target_pairs={{0,8},{8,16},{16,24},{24,0},{1,9},{9,17},{17,25},{25,1},{2,10},{10... | collective-permute-start | bytes 393224 | tf_op jit(solution)/shard_map/ppermute | solution.py:190
  8.5 1.1 collective-permute-start.2
  9.6 3.2 %collective-permute-start.1 = (bf16[4,64,256]{2,1,0:T(8,128)(2,1)S(1)}, bf16[4,64,256]{2,1,0:T(8,128)(2,1)S(1)}, u32[]{:S(2)}, u32[]{:S(2)}) collective-permute-start(bf16[4,64,256]{2,1,0:T(8,128)(2,1)S(1)} %get-tuple-element.49), channel_id=1, source_target_pairs={{1,0},{2,1},{3,2},{4,3},{5,4},{6,5},{7,6},{0,7},{9,8},{10,9},{11,1... | collective-permute-start | bytes 393224 | tf_op jit(solution)/shard_map/ppermute | solution.py:191
  12.8 0.8 slice_bitcast_fusion.17
  13.6 0.7 reshape.169
  14.3 0.7 compare_bitcast_fusion
  15.0 0.7 convert_bitcast_fusion
  15.7 0.6 fusion.21
  16.2 0.7 pad_clamp_fusion.1
  16.9 0.6 gather_fusion
  17.6 0.7 pad_clamp_fusion
  18.2 0.6 gather_fusion.1
  21.8 0.6 gather_fusion.3
  22.4 0.5 copy_select_fusion.1
  22.9 0.4 reverse_select_fusion.1
  23.2 0.7 fusion.2
  24.8 63.0 %shard_map.129 = (bf16[4,64,64,256]{3,2,1,0:T(8,128)(2,1)}, f32[4,64,256]{2,1,0:T(8,128)S(1)}, f32[4,64,256]{2,1,0:T(8,128)S(1)}, f32[4,64,1,256]{3,2,1,0:T(1,12...) custom-call(bf16[4,64,64,256]{3,2,1,0:T(8,128)(2,1)} %x_ref.1, bf16[4,64,64,256]{3,2,1,0:T(8,128)(2,1)} %cot_ref.1, ...), custom_call_target="tpu_custom_call" | custom-call | flops 4294967296 | bytes 25165824 | tf_op jit(solution)/shard_map/pallas_call | solution.py:544
  88.2 1.0 pad_maximum_fusion
  89.1 1.2 add_convert_fusion
  90.4 0.6 gather_fusion.4
  91.1 23.6 %shard_map.130 = (bf16[4,256,256]{2,1,0:T(8,128)(2,1)S(1)}, f32[256,256]{1,0:T(8,128)S(1)}, f32[9,256]{1,0:T(8,128)S(1)}, f32[1,256]{1,0:T(1,128)S(1)}) custom-call(bf16[4,256,256]{2,1,0:T(8,128)(2,1)S(1)} %bitcast.117, f32[272,256]{1,0:T(8,128)S(1)} %get-tuple-element.20.sums_ref), custom_call_target="tpu_custom_call" | custom-call | tf_op jit(solution)/shard_map/pallas_call | solution.py:428
  114.7 0.6 gather_fusion.5
  115.3 0.5 copy_select_fusion
  116.1 0.8 fusion
  116.9 17.9 %shard_map.131 = bf16[4,64,64,256]{3,2,1,0:T(8,128)(2,1)} custom-call(bf16[4,64,64,256]{3,2,1,0:T(8,128)(2,1)} %get-tuple-element.15.g_ref, bf16[4,64,256]{2,1,0:T(8,128)(2,1)S(1)} %bitcast.119, bf16[4,64,256]{2,1,0:T(8,128)(2,1)S(1)} %bitcast.118, f32[4,64,1,256]{3,2,1,0:T(1,128)S(1)} %get-tuple-element.36.west_ref, ...), custom_call_target="tpu_custom_call" | custom-call | flops 167772160 | bytes 16777216 | tf_op jit(solution)/shard_map/pallas_call | solution.py:611
  134.8 0.6 copy.85
  135.4 0.6 copy.86
  136.0 0.7 copy.87
  (51 shorter events, 2.3 us)
Async XLA Ops:
  5.5 16.2 %collective-permute-start = (bf16[4,64,256]{2,1,0:T(8,128)(2,1)S(1)}, bf16[4,64,256]{2,1,0:T(8,128)(2,1)S(1)}, u32[]{:S(2)}, u32[]{:S(2)}) collective-permute-start(bf16[4,64,256]{2,1,0:T(8,128)(2,1)S(1)} %get-tuple-element.46), channel_id=1, source_target_pairs={{0,8},{8,16},{16,24},{24,0},{1,9},{9,17},{17,25},{25,1},{2,10},{10... | collective-permute-start | bytes 393224 | tf_op jit(solution)/shard_map/ppermute | solution.py:190
  8.5 13.2 %collective-permute-start.3 = (bf16[4,64,256]{2,1,0:T(8,128)(2,1)S(1)}, bf16[4,64,256]{2,1,0:T(8,128)(2,1)S(1)}, u32[]{:S(2)}, u32[]{:S(2)}) collective-permute-start(bf16[4,64,256]{2,1,0:T(8,128)(2,1)S(1)} %get-tuple-element.47), channel_id=1, source_target_pairs={{0,1},{1,2},{2,3},{3,4},{4,5},{5,6},{6,7},{7,0},{8,9},{9,10},{10,1... | collective-permute-start | bytes 393224 | tf_op jit(solution)/shard_map/ppermute | solution.py:193
  8.5 13.2 %collective-permute-start.2 = (bf16[4,64,256]{2,1,0:T(8,128)(2,1)S(1)}, bf16[4,64,256]{2,1,0:T(8,128)(2,1)S(1)}, u32[]{:S(2)}, u32[]{:S(2)}) collective-permute-start(bf16[4,64,256]{2,1,0:T(8,128)(2,1)S(1)} %get-tuple-element.48), channel_id=1, source_target_pairs={{8,0},{16,8},{24,16},{0,24},{9,1},{17,9},{25,17},{1,25},{10,2},{18... | collective-permute-start | bytes 393224 | tf_op jit(solution)/shard_map/ppermute | solution.py:192
  9.6 12.1 %collective-permute-start.1 = (bf16[4,64,256]{2,1,0:T(8,128)(2,1)S(1)}, bf16[4,64,256]{2,1,0:T(8,128)(2,1)S(1)}, u32[]{:S(2)}, u32[]{:S(2)}) collective-permute-start(bf16[4,64,256]{2,1,0:T(8,128)(2,1)S(1)} %get-tuple-element.49), channel_id=1, source_target_pairs={{1,0},{2,1},{3,2},{4,3},{5,4},{6,5},{7,6},{0,7},{9,8},{10,9},{11,1... | collective-permute-start | bytes 393224 | tf_op jit(solution)/shard_map/ppermute | solution.py:191
  18.9 5.9 %copy-start = (f32[9,256]{1,0:T(8,128)S(1)}, f32[9,256]{1,0:T(8,128)}, u32[]{:S(2)}) copy-start(f32[9,256]{1,0:T(8,128)} %taps_ref.3) | copy-start | bytes 27652
  18.9 5.9 %copy-start.1 = (bf16[256,256]{1,0:T(8,128)(2,1)S(1)}, bf16[256,256]{1,0:T(8,128)(2,1)}, u32[]{:S(2)}) copy-start(bf16[256,256]{1,0:T(8,128)(2,1)} %point_ref.1) | copy-start | bytes 393220
  18.9 5.9 %copy-start.2 = (f32[256]{0:T(256)S(1)}, f32[256]{0:T(256)}, u32[]{:S(2)}) copy-start(f32[256]{0:T(256)} %param.16) | copy-start | bytes 3076
where the time goes:
time: 137 us
  Pallas kernels  104 us (76%)
  local copies, waits for them, and re-layouts  11.3 us (8%)
  other arithmetic  9.92 us (7%)
  starting transfers between devices  7.28 us (5%)
  between operations  3.71 us (3%)
    pallas_call x1, Pallas kernels, shards(): pl.pallas_call(functools.partial(first_kernel, norm_scale), grid=(batch,...  63 us
    pallas_call x1, Pallas kernels, return_and_sum(): pl.pallas_call(functools.partial(comm_kernel, face_count, tile_count), in...  23.6 us
    pallas_call x1, Pallas kernels, shards(): pl.pallas_call(second_kernel, grid=(batch,), in_specs=[whole, flat, flat,...  17.9 us
    ppermute x1, starting transfers between devices, exchange(): lax.ppermute(by_dir[3], 'tile', left)  3.2 us
    ppermute x1, starting transfers between devices, exchange(): lax.ppermute(by_dir[2], 'face', up)  2.99 us
  transfers between devices with their start and end apart: 4, of which 0 were waited for; matrix products, arithmetic and copies ran while one was open for 5% of the time, Pallas kernels for 0%

commit v1 on v0

--- a/solution.py
+++ b/solution.py
@@ -26,13 +26,26 @@
     return output, slope
 
 
+def rim_of_side(by_dir_ref, links_ref, s):
+    rows = by_dir_ref[links_ref[0, s], 0]
+    side = rows.shape[0]
+    spots = [lax.broadcasted_iota(jnp.int32, (side, side), axis) for axis in range(2)]
+    swap = jnp.where(spots[0] + spots[1] == side - 1, 1.0, 0.0).astype(BF16)
+    turned = jnp.dot(swap, rows, preferred_element_type=F32)
+    return jnp.where(jnp.full(rows.shape, links_ref[1, s]) == 1, turned, rows.astype(F32))
+
+
+def into_lines(lines_ref, rows):
+    for i in range(rows.shape[0]):
+        lines_ref[i] = rows[i : i + 1]
+
+
 def first_kernel(
     norm_scale,
     x_ref,
     cot_ref,
-    ends_ref,
-    west_ref,
-    east_ref,
+    rims_ref,
+    links_ref,
     taps_ref,
     bias_ref,
     point_ref,
@@ -46,6 +59,8 @@
     grad_act,
     act,
     parts,
+    west,
+    east,
 ):
     sample, step = pl.program_id(0), pl.program_id(1)
     side, channels = x_ref.shape[1], x_ref.shape[3]
@@ -53,9 +68,26 @@
 
     @pl.when(step == 0)
     def _():
-        for col_off in range(3):
-            win[col_off, 0] = ends_ref[0, 0, col_off].astype(F32)
-            win[col_off, side + 1] = ends_ref[0, 1, col_off].astype(F32)
+        rims = [rim_of_side(rims_ref, links_ref, s) for s in range(4)]
+        into_lines(west, rims[3])
+        into_lines(east, rims[1])
+
+        def corner(c, one, other):
+            mask = jnp.full((1, channels), links_ref[2, c]).astype(F32)
+            return (mask * 0.5 * (one + other)).astype(BF16).astype(F32)
+
+        north_west = corner(0, rims[0][:1], rims[3][:1])
+        north_east = corner(1, rims[0][side - 1 :], rims[1][:1])
+        south_east = corner(2, rims[1][side - 1 :], rims[2][side - 1 :])
+        south_west = corner(3, rims[2][:1], rims[3][side - 1 :])
+        spot = lax.broadcasted_iota(jnp.int32, (side, channels), 0)
+        for at, rim, low, high in (
+            (0, rims[0], north_west, north_east),
+            (side + 1, rims[2], south_west, south_east),
+        ):
+            win[0, at] = jnp.where(spot == 0, low, pltpu.roll(rim, 1, 0))
+            win[1, at] = rim
+            win[2, at] = jnp.where(spot == side - 1, high, pltpu.roll(rim, side - 1, 0))
         spot = lax.broadcasted_iota(jnp.int32, (side, HALF), 0)
         for lane in range(0, channels, HALF):
             lanes = pl.ds(lane, HALF)
@@ -64,10 +96,10 @@
                 mid = x_ref[0, i, :, lanes].astype(F32)
                 win[1, i + 1, :, lanes] = mid
                 win[0, i + 1, :, lanes] = jnp.where(
-                    spot == 0, west_ref[0, i, :, lanes], pltpu.roll(mid, 1, 0)
+                    spot == 0, west[i, :, lanes], pltpu.roll(mid, 1, 0)
                 )
                 win[2, i + 1, :, lanes] = jnp.where(
-                    spot == side - 1, east_ref[0, i, :, lanes], pltpu.roll(mid, side - 1, 0)
+                    spot == side - 1, east[i, :, lanes], pltpu.roll(mid, side - 1, 0)
                 )
                 return carry
 
@@ -138,8 +170,12 @@
         sums_ref[...] = sums_ref[...] * norm_scale
 
 
-def second_kernel(g_ref, north_ref, south_ref, west_ref, east_ref, taps_ref, out_ref):
+def second_kernel(g_ref, rims_ref, links_ref, taps_ref, out_ref, north, south, west, east):
     side, channels = g_ref.shape[1], g_ref.shape[3]
+    north[...] = rim_of_side(rims_ref, links_ref, 0)
+    into_lines(east, rim_of_side(rims_ref, links_ref, 1))
+    south[...] = rim_of_side(rims_ref, links_ref, 2)
+    into_lines(west, rim_of_side(rims_ref, links_ref, 3))
     spot = lax.broadcasted_iota(jnp.int32, (side, HALF), 0)
     for lane in range(0, channels, HALF):
         lanes = pl.ds(lane, HALF)
@@ -152,10 +188,10 @@
                 for c in range(3)
             ]
             from_right = jnp.where(
-                spot == side - 1, east_ref[0, i, :, lanes], pltpu.roll(cols[0], side - 1, 0)
+                spot == side - 1, east[i, :, lanes], pltpu.roll(cols[0], side - 1, 0)
             )
             from_left = jnp.where(
-                spot == 0, west_ref[0, i, :, lanes], pltpu.roll(cols[2], 1, 0)
+                spot == 0, west[i, :, lanes], pltpu.roll(cols[2], 1, 0)
             )
             return cols[1] + from_right + from_left
 
@@ -165,7 +201,7 @@
         empty = jnp.zeros((side, HALF), F32)
         first, second = load(0), load(1)
         out_ref[0, 0, :, lanes] = (
-            mixed(0, empty, first, second) + north_ref[0, :, lanes].astype(F32)
+            mixed(0, empty, first, second) + north[:, lanes]
         ).astype(BF16)
 
         def row(i, held):
@@ -175,7 +211,7 @@
 
         before, here = lax.fori_loop(1, side - 1, row, (first, second))
         out_ref[0, side - 1, :, lanes] = (
-            mixed(side - 1, before, here, empty) + south_ref[0, :, lanes].astype(F32)
+            mixed(side - 1, before, here, empty) + south[:, lanes]
         ).astype(BF16)
 
 
@@ -456,27 +492,6 @@
     )(leaving, sums)
 
 
-def window_rows(first, row, last):
-    row = jnp.concatenate([first[:, None], row, last[:, None]], axis=1)
-    side = row.shape[1] - 2
-    return jnp.stack([row[:, c : c + side] for c in range(3)], axis=1)
-
-
-def end_windows(rim_rows, cmask):
-    rim32 = rim_rows.astype(F32)
-    north_west = (cmask[0] * 0.5 * (rim32[0][:, 0] + rim32[3][:, 0])).astype(BF16)
-    north_east = (cmask[1] * 0.5 * (rim32[0][:, -1] + rim32[1][:, 0])).astype(BF16)
-    south_east = (cmask[2] * 0.5 * (rim32[1][:, -1] + rim32[2][:, -1])).astype(BF16)
-    south_west = (cmask[3] * 0.5 * (rim32[2][:, 0] + rim32[3][:, -1])).astype(BF16)
-    return jnp.stack(
-        [
-            window_rows(north_west, rim_rows[0], north_east),
-            window_rows(south_west, rim_rows[2], south_east),
-        ],
-        axis=1,
-    )
-
-
 def rim_terms(tap_rows, edges, mask_low, mask_high):
     length = edges.shape[2]
     spot = lax.broadcasted_iota(jnp.int32, (1, 1, length, 1), 2)
@@ -520,19 +535,14 @@
     counter = jnp.arange(4, dtype=jnp.int32)
     dir_of_side = jnp.sum(jnp.where(matched, counter[None, :], 0), axis=1)
     side_of_dir = jnp.sum(jnp.where(matched, counter[:, None], 0), axis=0)
-    flip_side = (link_flips[0] == 1)[:, None, None, None]
     cmask = corner_masks[0].astype(F32)
     norm_scale = float(batch * side * side * face_count * tile_count) ** (-0.5)
 
-    def toward_sides(by_dir):
-        got = jnp.take(by_dir, dir_of_side, axis=0)
-        return jnp.where(flip_side, got[:, :, ::-1], got)
-
     edges = jnp.stack(
         [state_field[:, 0], state_field[:, :, -1], state_field[:, -1], state_field[:, :, 0]]
     )
-    rim_rows = toward_sides(exchange(jnp.take(edges, side_of_dir, axis=0)))
-    ends = end_windows(rim_rows, cmask)
+    rims = exchange(jnp.take(edges, side_of_dir, axis=0))
+    links = jnp.stack([dir_of_side, link_flips[0], corner_masks[0]])
 
     whole = pl.BlockSpec((1, side, side, channels), lambda b, s: (b, 0, 0, 0))
     rows_of = pl.BlockSpec((1, ROWS, side, channels), lambda b, s: (b, s, 0, 0))
@@ -547,9 +557,8 @@
         in_specs=[
             whole,
             rows_of,
-            pl.BlockSpec((1, 2, 3, side, channels), lambda b, s: (b, 0, 0, 0, 0)),
-            line,
-            line,
+            pl.BlockSpec((4, 1, side, channels), lambda b, s: (0, b, 0, 0)),
+            pl.BlockSpec(memory_space=pltpu.SMEM),
             fixed(9, channels),
             fixed(1, channels),
             fixed(channels, channels),
@@ -568,6 +577,8 @@
             pltpu.VMEM((ROWS, side, channels), F32),
             pltpu.VMEM((ROWS, side, channels), BF16),
             pltpu.VMEM((10, 8, channels), F32),
+            pltpu.VMEM((side, 1, channels), F32),
+            pltpu.VMEM((side, 1, channels), F32),
         ],
         compiler_params=pltpu.CompilerParams(vmem_limit_bytes=48 * 2**20),
         cost_estimate=pl.CostEstimate(
@@ -578,9 +589,8 @@
     )(
         state_field,
         cotangent,
-        ends,
-        rim_rows[3].astype(F32)[:, :, None],
-        rim_rows[1].astype(F32)[:, :, None],
+        rims,
+        links,
         depth_weight,
         depth_bias[None],
         point_weight,
@@ -603,16 +613,24 @@
     returned, point_sum, depth_sum, bias_sum = return_and_sum(
         leaving.reshape(4, batch * side, channels), sums
     )
-    incoming = toward_sides(returned.reshape(leaving.shape))
 
     whole = pl.BlockSpec((1, side, side, channels), lambda b: (b, 0, 0, 0))
-    line = pl.BlockSpec((1, side, 1, channels), lambda b: (b, 0, 0, 0))
-    flat = pl.BlockSpec((1, side, channels), lambda b: (b, 0, 0))
     field_grad = pl.pallas_call(
         second_kernel,
         grid=(batch,),
-        in_specs=[whole, flat, flat, line, line, pl.BlockSpec((9, channels), lambda b: (0, 0))],
+        in_specs=[
+            whole,
+            pl.BlockSpec((4, 1, side, channels), lambda b: (0, b, 0, 0)),
+            pl.BlockSpec(memory_space=pltpu.SMEM),
+            pl.BlockSpec((9, channels), lambda b: (0, 0)),
+        ],
         out_specs=whole,
+        scratch_shapes=[
+            pltpu.VMEM((side, channels), F32),
+            pltpu.VMEM((side, channels), F32),
+            pltpu.VMEM((side, 1, channels), F32),
+            pltpu.VMEM((side, 1, channels), F32),
+        ],
         out_shape=jax.ShapeDtypeStruct(state_field.shape, BF16),
         compiler_params=pltpu.CompilerParams(vmem_limit_bytes=48 * 2**20),
         cost_estimate=pl.CostEstimate(
@@ -622,10 +640,8 @@
         ),
     )(
         grad_hidden,
-        incoming[0],
-        incoming[2],
-        incoming[3].astype(F32)[:, :, None],
-        incoming[1].astype(F32)[:, :, None],
+        returned.reshape(leaving.shape),
+        links,
         depth_weight,
     )
     return field_grad, depth_sum, bias_sum[0], point_sum

time: 137 us -> 131 us (0.956)
  other arithmetic: 9.92 us -> 6.32 us
  Pallas kernels: 104 us -> 107 us
  between operations: 3.71 us -> 0.92 us
  local copies, waits for them, and re-layouts: 11.3 us -> 9.35 us
    select_n x8 -> x2, other arithmetic: 1.93 us -> 0.12 us  [shards(): rims = exchange(jnp.take(edges, side_of_dir, axis=0))]
    convert_element_type x3 -> x0, other arithmetic: 1.54 us -> none  [the longest x1 0.76 us: shards(): incoming[1].astype(F32)[:, :, None]]
  transfers between devices with their start and end apart: 4 -> 4, of which waited for: 0 -> 0; matrix products, arithmetic and copies ran while one was open for 5% -> 4% of each run, Pallas kernels for 0% -> 0%
where the time goes in v1:
time: 131 us
  Pallas kernels  107 us (82%)
  local copies, waits for them, and re-layouts  9.35 us (7%)
  starting transfers between devices  7.28 us (6%)
  other arithmetic  6.32 us (5%)
    pallas_call x1, Pallas kernels, shards(): pl.pallas_call(functools.partial(first_kernel, norm_scale), grid=(batch,...  64.4 us
    pallas_call x1, Pallas kernels, return_and_sum(): pl.pallas_call(functools.partial(comm_kernel, face_count, tile_count), in...  23.6 us
    pallas_call x1, Pallas kernels, shards(): pl.pallas_call(second_kernel, grid=(batch,), in_specs=[whole, pl.BlockSpe...  18.8 us
    ppermute x1, starting transfers between devices, exchange(): lax.ppermute(by_dir[3], 'tile', left)  3.2 us
    ppermute x1, starting transfers between devices, exchange(): lax.ppermute(by_dir[2], 'face', up)  2.99 us
  transfers between devices with their start and end apart: 4, of which 0 were waited for; matrix products, arithmetic and copies ran while one was open for 4% of the time, Pallas kernels for 0%

profile of v1, /device:TPU:0, one launch (start us, length us, event | category | flops | bytes accessed | tf_op | source)
XLA Modules:
  0.0 130.6 jit_solution(3337601725630172558)
XLA Ops:
  0.7 0.1 pad_add_fusion.1
  0.8 0.8 fusion.1
  1.7 1.0 slice_bitcast_fusion.5
  2.7 2.0 %fusion.2 = (bf16[4,64,1,256]{3,2,1,0:T(2,128)(2,1)S(1)}, bf16[4,64,1,256]{3,2,1,0:T(2,128)(2,1)S(1)}) fusion(bf16[4,64,64,256]{3,2,1,0:T(8,128)(2,1)} %x_ref.1), kind=kLoop, calls=%fused_computation.48 | loop fusion | bytes 524288 | tf_op jit(solution)/shard_map/slice | solution.py:542
  4.7 0.1 pad_maximum_fusion.1
  4.8 0.6 gather_fusion.2
  5.4 0.1 broadcast_select_fusion.1
  5.5 3.0 %collective-permute-start = (bf16[4,64,256]{2,1,0:T(8,128)(2,1)S(1)}, bf16[4,64,256]{2,1,0:T(8,128)(2,1)S(1)}, u32[]{:S(2)}, u32[]{:S(2)}) collective-permute-start(bf16[4,64,256]{2,1,0:T(8,128)(2,1)S(1)} %get-tuple-element.31), channel_id=1, source_target_pairs={{0,8},{8,16},{16,24},{24,0},{1,9},{9,17},{17,25},{25,1},{2,10},{10... | collective-permute-start | bytes 393224 | tf_op jit(solution)/shard_map/ppermute | solution.py:226
  8.5 1.1 collective-permute-start.2
  9.6 3.2 %collective-permute-start.1 = (bf16[4,64,256]{2,1,0:T(8,128)(2,1)S(1)}, bf16[4,64,256]{2,1,0:T(8,128)(2,1)S(1)}, u32[]{:S(2)}, u32[]{:S(2)}) collective-permute-start(bf16[4,64,256]{2,1,0:T(8,128)(2,1)S(1)} %get-tuple-element.34), channel_id=1, source_target_pairs={{1,0},{2,1},{3,2},{4,3},{5,4},{6,5},{7,6},{0,7},{9,8},{10,9},{11,1... | collective-permute-start | bytes 393224 | tf_op jit(solution)/shard_map/ppermute | solution.py:227
  12.8 0.8 slice_bitcast_fusion.7
  13.6 0.7 reshape.90
  14.3 0.7 convert_bitcast_fusion
  15.0 0.7 pad_clamp_fusion.1
  15.6 0.6 gather_fusion
  16.3 0.7 pad_clamp_fusion
  17.0 0.6 gather_fusion.1
  17.6 0.1 broadcast_multiply_fusion.1
  17.8 0.7 pad_add_fusion.links_ref
  18.6 64.4 %shard_map.129 = (bf16[4,64,64,256]{3,2,1,0:T(8,128)(2,1)}, f32[4,64,256]{2,1,0:T(8,128)S(1)}, f32[4,64,256]{2,1,0:T(8,128)S(1)}, f32[4,64,1,256]{3,2,1,0:T(1,12...) custom-call(bf16[4,64,64,256]{3,2,1,0:T(8,128)(2,1)} %x_ref.1, bf16[4,64,64,256]{3,2,1,0:T(8,128)(2,1)} %cot_ref.1, ...), custom_call_target="tpu_custom_call" | custom-call | flops 4294967296 | bytes 25165824 | tf_op jit(solution)/shard_map/pallas_call | solution.py:554
  83.0 0.2 stack.65
  83.2 0.2 stack.66
  83.4 1.0 pad_maximum_fusion
  84.4 1.2 add_convert_fusion
  85.6 0.1 copy.31
  85.6 0.6 gather_fusion.3
  86.2 0.1 broadcast_select_fusion
  86.4 23.6 %shard_map.130 = (bf16[4,256,256]{2,1,0:T(8,128)(2,1)S(1)}, f32[256,256]{1,0:T(8,128)S(1)}, f32[9,256]{1,0:T(8,128)S(1)}, f32[1,256]{1,0:T(1,128)S(1)}) custom-call(bf16[4,256,256]{2,1,0:T(8,128)(2,1)S(1)} %bitcast.57, f32[272,256]{1,0:T(8,128)S(1)} %get-tuple-element.20.sums_ref), custom_call_target="tpu_custom_call" | custom-call | tf_op jit(solution)/shard_map/pallas_call | solution.py:464
  109.9 18.8 %shard_map.131 = bf16[4,64,64,256]{3,2,1,0:T(8,128)(2,1)} custom-call(bf16[4,64,64,256]{3,2,1,0:T(8,128)(2,1)} %get-tuple-element.15.g_ref, bf16[4,4,64,256]{3,2,1,0:T(8,128)(2,1)S(1)} %bitcast.58, s32[3,4]{1,0:T(4,128)S(1)} %pad_add_fusion.links_ref, f32[9,256]{1,0:T(8,128)S(1)} %copy-done), custom_call_target="tpu_custom_call" | custom-call | flops 167772160 | bytes 16777216 | tf_op jit(solution)/shard_map/pallas_call | solution.py:618
  128.8 0.6 copy.57
  129.4 0.6 copy.58
  129.9 0.7 copy.59
  (27 shorter events, 0.3 us)
Async XLA Ops:
  0.6 18.0 %copy-start = (f32[9,256]{1,0:T(8,128)S(1)}, f32[9,256]{1,0:T(8,128)}, u32[]{:S(2)}) copy-start(f32[9,256]{1,0:T(8,128)} %taps_ref.3) | copy-start | bytes 27652
  0.6 18.0 %copy-start.1 = (bf16[256,256]{1,0:T(8,128)(2,1)S(1)}, bf16[256,256]{1,0:T(8,128)(2,1)}, u32[]{:S(2)}) copy-start(bf16[256,256]{1,0:T(8,128)(2,1)} %point_ref.1) | copy-start | bytes 393220
  0.7 18.0 %copy-start.2 = (f32[256]{0:T(256)S(1)}, f32[256]{0:T(256)}, u32[]{:S(2)}) copy-start(f32[256]{0:T(256)} %param.16) | copy-start | bytes 3076
  5.5 13.0 %collective-permute-start = (bf16[4,64,256]{2,1,0:T(8,128)(2,1)S(1)}, bf16[4,64,256]{2,1,0:T(8,128)(2,1)S(1)}, u32[]{:S(2)}, u32[]{:S(2)}) collective-permute-start(bf16[4,64,256]{2,1,0:T(8,128)(2,1)S(1)} %get-tuple-element.31), channel_id=1, source_target_pairs={{0,8},{8,16},{16,24},{24,0},{1,9},{9,17},{17,25},{25,1},{2,10},{10... | collective-permute-start | bytes 393224 | tf_op jit(solution)/shard_map/ppermute | solution.py:226
  8.5 10.0 %collective-permute-start.3 = (bf16[4,64,256]{2,1,0:T(8,128)(2,1)S(1)}, bf16[4,64,256]{2,1,0:T(8,128)(2,1)S(1)}, u32[]{:S(2)}, u32[]{:S(2)}) collective-permute-start(bf16[4,64,256]{2,1,0:T(8,128)(2,1)S(1)} %get-tuple-element.32), channel_id=1, source_target_pairs={{0,1},{1,2},{2,3},{3,4},{4,5},{5,6},{6,7},{7,0},{8,9},{9,10},{10,1... | collective-permute-start | bytes 393224 | tf_op jit(solution)/shard_map/ppermute | solution.py:229
  8.5 10.0 %collective-permute-start.2 = (bf16[4,64,256]{2,1,0:T(8,128)(2,1)S(1)}, bf16[4,64,256]{2,1,0:T(8,128)(2,1)S(1)}, u32[]{:S(2)}, u32[]{:S(2)}) collective-permute-start(bf16[4,64,256]{2,1,0:T(8,128)(2,1)S(1)} %get-tuple-element.33), channel_id=1, source_target_pairs={{8,0},{16,8},{24,16},{0,24},{9,1},{17,9},{25,17},{1,25},{10,2},{18... | collective-permute-start | bytes 393224 | tf_op jit(solution)/shard_map/ppermute | solution.py:228
  9.6 8.9 %collective-permute-start.1 = (bf16[4,64,256]{2,1,0:T(8,128)(2,1)S(1)}, bf16[4,64,256]{2,1,0:T(8,128)(2,1)S(1)}, u32[]{:S(2)}, u32[]{:S(2)}) collective-permute-start(bf16[4,64,256]{2,1,0:T(8,128)(2,1)S(1)} %get-tuple-element.34), channel_id=1, source_target_pairs={{1,0},{2,1},{3,2},{4,3},{5,4},{6,5},{7,6},{0,7},{9,8},{10,9},{11,1... | collective-permute-start | bytes 393224 | tf_op jit(solution)/shard_map/ppermute | solution.py:227

commit v2 on v1

--- a/solution.py
+++ b/solution.py
@@ -50,10 +50,7 @@
     bias_ref,
     point_ref,
     g_ref,
-    gnorth_ref,
-    gsouth_ref,
-    gwest_ref,
-    geast_ref,
+    leaving_ref,
     sums_ref,
     win,
     grad_act,
@@ -61,6 +58,9 @@
     parts,
     west,
     east,
+    gwest,
+    geast,
+    gedges,
 ):
     sample, step = pl.program_id(0), pl.program_id(1)
     side, channels = x_ref.shape[1], x_ref.shape[3]
@@ -136,9 +136,9 @@
                 g_ref[0, k, spots, lanes] = grad
                 grad = grad.astype(F32)
                 if low == 0:
-                    gwest_ref[0, i, :, lanes] = grad[:1]
+                    gwest[i, :, lanes] = grad[:1]
                 if low + STRIP == side:
-                    geast_ref[0, i, :, lanes] = grad[STRIP - 1 :]
+                    geast[i, :, lanes] = grad[STRIP - 1 :]
                 for t in range(9):
                     term = grad * views[t]
                     held[t] = held[t] + (term[:8] + term[8:])
@@ -157,11 +157,32 @@
 
     @pl.when(step == 0)
     def _():
-        gnorth_ref[0] = g_ref[0, 0].astype(F32)
+        gedges[0] = g_ref[0, 0].astype(F32)
 
     @pl.when(step == pl.num_programs(1) - 1)
     def _():
-        gsouth_ref[0] = g_ref[0, rows - 1].astype(F32)
+        gedges[2] = g_ref[0, rows - 1].astype(F32)
+        for i in range(side):
+            gedges[1, i : i + 1] = geast[i]
+            gedges[3, i : i + 1] = gwest[i]
+        spot = lax.broadcasted_iota(jnp.int32, (side, channels), 0)
+        for s, (first, middle, last, low, high) in enumerate(
+            [(0, 1, 2, 0, 1), (2, 5, 8, 1, 2), (6, 7, 8, 3, 2), (0, 3, 6, 0, 3)]
+        ):
+            edge = gedges[s]
+            share = [
+                0.5 * jnp.full((1, channels), links_ref[2, c]).astype(F32) for c in (low, high)
+            ]
+            onward = taps_ref[first : first + 1, :] * jnp.where(
+                spot == side - 1, 0.0, pltpu.roll(edge, side - 1, 0)
+            )
+            back = taps_ref[last : last + 1, :] * jnp.where(spot == 0, 0.0, pltpu.roll(edge, 1, 0))
+            ends = jnp.where(spot == 0, share[0] * taps_ref[first : first + 1, :] * edge, 0.0)
+            ends = ends + jnp.where(
+                spot == side - 1, share[1] * taps_ref[last : last + 1, :] * edge, 0.0
+            )
+            rim = onward + taps_ref[middle : middle + 1, :] * edge + back + ends
+            leaving_ref[links_ref[0, s], 0] = rim.astype(BF16)
 
     @pl.when((step == pl.num_programs(1) - 1) & (sample == pl.num_programs(0) - 1))
     def _():
@@ -492,21 +513,6 @@
     )(leaving, sums)
 
 
-def rim_terms(tap_rows, edges, mask_low, mask_high):
-    length = edges.shape[2]
-    spot = lax.broadcasted_iota(jnp.int32, (1, 1, length, 1), 2)
-    padded_rows = jnp.pad(edges, ((0, 0), (0, 0), (1, 1), (0, 0)))
-    tap_first = tap_rows[:, 0][:, None, None, :]
-    tap_middle = tap_rows[:, 1][:, None, None, :]
-    tap_last = tap_rows[:, 2][:, None, None, :]
-    return (
-        (tap_first * padded_rows[:, :, 2:] + tap_middle * edges)
-        + tap_last * padded_rows[:, :, :-2]
-        + jnp.where(spot == 0, (0.5 * mask_low) * tap_first * edges, 0.0)
-        + jnp.where(spot == length - 1, (0.5 * mask_high) * tap_last * edges, 0.0)
-    )
-
-
 def shards(
     state_field,
     cotangent,
@@ -535,7 +541,6 @@
     counter = jnp.arange(4, dtype=jnp.int32)
     dir_of_side = jnp.sum(jnp.where(matched, counter[None, :], 0), axis=1)
     side_of_dir = jnp.sum(jnp.where(matched, counter[:, None], 0), axis=0)
-    cmask = corner_masks[0].astype(F32)
     norm_scale = float(batch * side * side * face_count * tile_count) ** (-0.5)
 
     edges = jnp.stack(
@@ -546,12 +551,10 @@
 
     whole = pl.BlockSpec((1, side, side, channels), lambda b, s: (b, 0, 0, 0))
     rows_of = pl.BlockSpec((1, ROWS, side, channels), lambda b, s: (b, s, 0, 0))
-    line = pl.BlockSpec((1, side, 1, channels), lambda b, s: (b, 0, 0, 0))
-    flat = pl.BlockSpec((1, side, channels), lambda b, s: (b, 0, 0))
     fixed = lambda *shape: pl.BlockSpec(shape, lambda b, s: (0,) * len(shape))
     pixels = batch * side * side
     sum_rows = channels + 16
-    grad_hidden, grad_north, grad_south, grad_west, grad_east, sums = pl.pallas_call(
+    grad_hidden, leaving, sums = pl.pallas_call(
         functools.partial(first_kernel, norm_scale),
         grid=(batch, side // ROWS),
         in_specs=[
@@ -563,13 +566,14 @@
             fixed(1, channels),
             fixed(channels, channels),
         ],
-        out_specs=[rows_of, flat, flat, line, line, fixed(sum_rows, channels)],
+        out_specs=[
+            rows_of,
+            pl.BlockSpec((4, 1, side, channels), lambda b, s: (0, b, 0, 0)),
+            fixed(sum_rows, channels),
+        ],
         out_shape=[
             jax.ShapeDtypeStruct(state_field.shape, BF16),
-            jax.ShapeDtypeStruct((batch, side, channels), F32),
-            jax.ShapeDtypeStruct((batch, side, channels), F32),
-            jax.ShapeDtypeStruct((batch, side, 1, channels), F32),
-            jax.ShapeDtypeStruct((batch, side, 1, channels), F32),
+            jax.ShapeDtypeStruct((4, batch, side, channels), BF16),
             jax.ShapeDtypeStruct((sum_rows, channels), F32),
         ],
         scratch_shapes=[
@@ -577,9 +581,9 @@
             pltpu.VMEM((ROWS, side, channels), F32),
             pltpu.VMEM((ROWS, side, channels), BF16),
             pltpu.VMEM((10, 8, channels), F32),
-            pltpu.VMEM((side, 1, channels), F32),
-            pltpu.VMEM((side, 1, channels), F32),
-        ],
+        ]
+        + [pltpu.VMEM((side, 1, channels), F32)] * 4
+        + [pltpu.VMEM((4, side, channels), F32)],
         compiler_params=pltpu.CompilerParams(vmem_limit_bytes=48 * 2**20),
         cost_estimate=pl.CostEstimate(
             flops=4 * pixels * channels * channels,
@@ -596,20 +600,6 @@
         point_weight,
     )
 
-    tap_table = depth_weight.reshape(3, 3, channels)
-    side_taps = jnp.stack([tap_table[0], tap_table[:, 2], tap_table[2], tap_table[:, 0]], axis=0)
-    mask_low = cmask[jnp.array([0, 1, 3, 0])][:, None, None, None]
-    mask_high = cmask[jnp.array([1, 2, 2, 3])][:, None, None, None]
-    grad_edges = jnp.stack(
-        [
-            grad_north,
-            grad_east[:, :, 0],
-            grad_south,
-            grad_west[:, :, 0],
-        ]
-    )
-    leaving = rim_terms(side_taps, grad_edges, mask_low, mask_high).astype(BF16)
-    leaving = jnp.take(leaving, side_of_dir, axis=0)
     returned, point_sum, depth_sum, bias_sum = return_and_sum(
         leaving.reshape(4, batch * side, channels), sums
     )

time: 131 us -> 128 us (0.977)
  other arithmetic: 6.32 us -> 1.87 us
  waiting for transfers between devices: 0.01 us -> 2.54 us
  local copies, waits for them, and re-layouts: 9.35 us -> 7.8 us
    unnamed x12 -> x11, local copies, waits for them, and re-layouts: 1.89 us -> 4.17 us
    gather x3 -> x0, local copies, waits for them, and re-layouts: 1.86 us -> none  [the longest x1 0.64 us: shards(): mask_high = cmask[jnp.array([1, 2, 2, 3])][:, None, None, None]]
    convert_element_type x2 -> x0, other arithmetic: 1.85 us -> none  [the longest x1 1.19 us: shards(): leaving = rim_terms(side_taps, grad_edges, mask_low, mask_high).astype(BF16)]
    gather x3 -> x1, other arithmetic: 1.33 us -> 0.01 us  [shards(): rims = exchange(jnp.take(edges, side_of_dir, axis=0))]
  transfers between devices with their start and end apart: 4 -> 4, of which waited for: 0 -> 2; matrix products, arithmetic and copies ran while one was open for 4% -> 1% of each run, Pallas kernels for 0% -> 0%
where the time goes in v2:
time: 128 us
  Pallas kernels  108 us (84%)
  local copies, waits for them, and re-layouts  7.8 us (6%)
  starting transfers between devices  7.28 us (6%)
  waiting for transfers between devices  2.54 us (2%)
  other arithmetic  1.87 us (1%)
    pallas_call x1, Pallas kernels, shards(): pl.pallas_call(functools.partial(first_kernel, norm_scale), grid=(batch,...  64.1 us
    pallas_call x1, Pallas kernels, return_and_sum(): pl.pallas_call(functools.partial(comm_kernel, face_count, tile_count), in...  24.6 us
    pallas_call x1, Pallas kernels, shards(): pl.pallas_call(second_kernel, grid=(batch,), in_specs=[whole, pl.BlockSpe...  18.8 us
    unnamed x11, local copies, waits for them, and re-layouts  4.17 us
    ppermute x1, starting transfers between devices, exchange(): lax.ppermute(by_dir[3], 'tile', left)  3.2 us
    ppermute x1, starting transfers between devices, exchange(): lax.ppermute(by_dir[2], 'face', up)  2.99 us
  transfers between devices with their start and end apart: 4, of which 2 were waited for; matrix products, arithmetic and copies ran while one was open for 1% of the time, Pallas kernels for 0%

profile of v2, /device:TPU:0, one launch (start us, length us, event | category | flops | bytes accessed | tf_op | source)
XLA Modules:
  0.0 127.9 jit_solution(9855706513042161570)
XLA Ops:
  0.7 0.1 pad_add_fusion.1
  0.8 0.8 fusion.1
  1.6 1.0 slice_bitcast_fusion.5
  2.6 2.0 %fusion.3 = (bf16[4,64,1,256]{3,2,1,0:T(2,128)(2,1)S(1)}, bf16[4,64,1,256]{3,2,1,0:T(2,128)(2,1)S(1)}) fusion(bf16[4,64,64,256]{3,2,1,0:T(8,128)(2,1)} %x_ref.1), kind=kLoop, calls=%fused_computation.23 | loop fusion | bytes 524288 | tf_op jit(solution)/shard_map/slice | solution.py:547
  4.7 0.1 pad_maximum_fusion
  4.7 0.6 gather_fusion
  5.3 0.1 broadcast_select_fusion
  5.5 3.0 %collective-permute-start = (bf16[4,64,256]{2,1,0:T(8,128)(2,1)S(1)}, bf16[4,64,256]{2,1,0:T(8,128)(2,1)S(1)}, u32[]{:S(2)}, u32[]{:S(2)}) collective-permute-start(bf16[4,64,256]{2,1,0:T(8,128)(2,1)S(1)} %get-tuple-element.24), channel_id=1, source_target_pairs={{0,8},{8,16},{16,24},{24,0},{1,9},{9,17},{17,25},{25,1},{2,10},{10... | collective-permute-start | bytes 393224 | tf_op jit(solution)/shard_map/ppermute | solution.py:247
  8.5 0.0 collective-permute-start.3
  8.5 1.1 collective-permute-start.2
  9.6 3.2 %collective-permute-start.1 = (bf16[4,64,256]{2,1,0:T(8,128)(2,1)S(1)}, bf16[4,64,256]{2,1,0:T(8,128)(2,1)S(1)}, u32[]{:S(2)}, u32[]{:S(2)}) collective-permute-start(bf16[4,64,256]{2,1,0:T(8,128)(2,1)S(1)} %get-tuple-element.27), channel_id=1, source_target_pairs={{1,0},{2,1},{3,2},{4,3},{5,4},{6,5},{7,6},{0,7},{9,8},{10,9},{11,1... | collective-permute-start | bytes 393224 | tf_op jit(solution)/shard_map/ppermute | solution.py:248
  12.8 0.7 pad_add_fusion.links_ref
  13.5 0.0 collective-permute-done
  13.5 1.2 collective-permute-done.3
  14.7 1.3 %collective-permute-done.2 = bf16[4,64,256]{2,1,0:T(8,128)(2,1)S(1)} collective-permute-done((bf16[4,64,256]{2,1,0:T(8,128)(2,1)S(1)}, bf16[4,64,256]{2,1,0:T(8,128)(2,1)S(1)}, u32[]{:S(2)}, u32[]{:S(2)}) %collective-permute-start.2) | collective-permute-done | bytes 131104 | tf_op jit(solution)/shard_map/ppermute | solution.py:249
  16.0 0.0 collective-permute-done.1
  16.0 0.1 pad_maximum_fusion.1.rims_ref
  16.1 0.0 copy-start
  16.1 0.9 copy-done
  17.0 0.0 copy-start.1
  17.0 0.7 copy-done.1
  17.7 0.0 copy-start.3
  17.7 0.7 copy-done.3
  18.4 0.0 copy-start.2
  18.4 64.1 %shard_map.111 = (bf16[4,64,64,256]{3,2,1,0:T(8,128)(2,1)}, bf16[4,4,64,256]{3,2,1,0:T(8,128)(2,1)S(1)}, f32[272,256]{1,0:T(8,128)S(1)}) custom-call(bf16[4,64,64,256]{3,2,1,0:T(8,128)(2,1)} %x_ref.1, bf16[4,64,64,256]{3,2,1,0:T(8,128)(2,1)} %cot_ref.1, bf16[4,4,64,256]{3,2,1,0:T(8,128)(2,1)S(1)} %pad_maximum_fusion.1.rims_ref, ...), custom_call_target="tpu_custom_call" | custom-call | flops 4294967296 | bytes 25165824 | tf_op jit(solution)/shard_map/pallas_call | solution.py:557
  82.5 24.6 %shard_map.112 = (bf16[4,256,256]{2,1,0:T(8,128)(2,1)S(1)}, f32[256,256]{1,0:T(8,128)S(1)}, f32[9,256]{1,0:T(8,128)S(1)}, f32[1,256]{1,0:T(1,128)S(1)}) custom-call(bf16[4,256,256]{2,1,0:T(8,128)(2,1)S(1)} %bitcast.36, f32[272,256]{1,0:T(8,128)S(1)} %get-tuple-element.13.sums_ref), custom_call_target="tpu_custom_call" | custom-call | tf_op jit(solution)/shard_map/pallas_call | solution.py:485
  107.1 0.0 copy-done.2
  107.1 18.8 %shard_map.113 = bf16[4,64,64,256]{3,2,1,0:T(8,128)(2,1)} custom-call(bf16[4,64,64,256]{3,2,1,0:T(8,128)(2,1)} %get-tuple-element.11.g_ref, bf16[4,4,64,256]{3,2,1,0:T(8,128)(2,1)S(1)} %bitcast.37, s32[3,4]{1,0:T(4,128)S(1)} %pad_add_fusion.links_ref, f32[9,256]{1,0:T(8,128)S(1)} %copy-done.2), custom_call_target="tpu_custom_call" | custom-call | flops 167772160 | bytes 16777216 | tf_op jit(solution)/shard_map/pallas_call | solution.py:608
  126.0 0.6 copy.26
  126.6 0.6 copy.27
  127.2 0.7 copy.28
  (5 shorter events, 0.1 us)
Async XLA Ops:
  5.5 8.0 %collective-permute-start = (bf16[4,64,256]{2,1,0:T(8,128)(2,1)S(1)}, bf16[4,64,256]{2,1,0:T(8,128)(2,1)S(1)}, u32[]{:S(2)}, u32[]{:S(2)}) collective-permute-start(bf16[4,64,256]{2,1,0:T(8,128)(2,1)S(1)} %get-tuple-element.24), channel_id=1, source_target_pairs={{0,8},{8,16},{16,24},{24,0},{1,9},{9,17},{17,25},{25,1},{2,10},{10... | collective-permute-start | bytes 393224 | tf_op jit(solution)/shard_map/ppermute | solution.py:247
  8.5 6.2 %collective-permute-start.3 = (bf16[4,64,256]{2,1,0:T(8,128)(2,1)S(1)}, bf16[4,64,256]{2,1,0:T(8,128)(2,1)S(1)}, u32[]{:S(2)}, u32[]{:S(2)}) collective-permute-start(bf16[4,64,256]{2,1,0:T(8,128)(2,1)S(1)} %get-tuple-element.25), channel_id=1, source_target_pairs={{0,1},{1,2},{2,3},{3,4},{4,5},{5,6},{6,7},{7,0},{8,9},{9,10},{10,1... | collective-permute-start | bytes 393224 | tf_op jit(solution)/shard_map/ppermute | solution.py:250
  8.5 7.5 %collective-permute-start.2 = (bf16[4,64,256]{2,1,0:T(8,128)(2,1)S(1)}, bf16[4,64,256]{2,1,0:T(8,128)(2,1)S(1)}, u32[]{:S(2)}, u32[]{:S(2)}) collective-permute-start(bf16[4,64,256]{2,1,0:T(8,128)(2,1)S(1)} %get-tuple-element.26), channel_id=1, source_target_pairs={{8,0},{16,8},{24,16},{0,24},{9,1},{17,9},{25,17},{1,25},{10,2},{18... | collective-permute-start | bytes 393224 | tf_op jit(solution)/shard_map/ppermute | solution.py:249
  9.6 6.4 %collective-permute-start.1 = (bf16[4,64,256]{2,1,0:T(8,128)(2,1)S(1)}, bf16[4,64,256]{2,1,0:T(8,128)(2,1)S(1)}, u32[]{:S(2)}, u32[]{:S(2)}) collective-permute-start(bf16[4,64,256]{2,1,0:T(8,128)(2,1)S(1)} %get-tuple-element.27), channel_id=1, source_target_pairs={{1,0},{2,1},{3,2},{4,3},{5,4},{6,5},{7,6},{0,7},{9,8},{10,9},{11,1... | collective-permute-start | bytes 393224 | tf_op jit(solution)/shard_map/ppermute | solution.py:248
  16.1 0.9 copy-start
  17.0 0.7 copy-start.1
  17.7 0.7 copy-start.3
  18.4 88.8 %copy-start.2 = (f32[9,256]{1,0:T(8,128)S(1)}, f32[9,256]{1,0:T(8,128)}, u32[]{:S(2)}) copy-start(f32[9,256]{1,0:T(8,128)} %taps_ref.3) | copy-start | bytes 27652

commit v3 on v2

--- a/solution.py
+++ b/solution.py
@@ -11,7 +11,7 @@
 cubic_coef = 0.044715
 HALF = 128
 STRIP = 16
-ROWS = 16
+ROWS = 32
 F32 = jnp.float32
 BF16 = jnp.bfloat16
 

time: 128 us -> 125 us (0.977)
  Pallas kernels: 108 us -> 104 us
    pallas_call x1, Pallas kernels: 64.1 us -> 61 us  [shards(): pl.pallas_call(functools.partial(first_kernel, norm_scale), grid=(batch,...]
where the time goes in v3:
time: 125 us
  Pallas kernels  104 us (83%)
  local copies, waits for them, and re-layouts  7.8 us (6%)
  starting transfers between devices  7.28 us (6%)
  waiting for transfers between devices  2.54 us (2%)
  other arithmetic  1.87 us (1%)
    pallas_call x1, Pallas kernels, shards(): pl.pallas_call(functools.partial(first_kernel, norm_scale), grid=(batch,...  61 us
    pallas_call x1, Pallas kernels, return_and_sum(): pl.pallas_call(functools.partial(comm_kernel, face_count, tile_count), in...  24.6 us
    pallas_call x1, Pallas kernels, shards(): pl.pallas_call(second_kernel, grid=(batch,), in_specs=[whole, pl.BlockSpe...  18.8 us
    unnamed x11, local copies, waits for them, and re-layouts  4.17 us
    ppermute x1, starting transfers between devices, exchange(): lax.ppermute(by_dir[3], 'tile', left)  3.2 us
    ppermute x1, starting transfers between devices, exchange(): lax.ppermute(by_dir[2], 'face', up)  2.99 us
  transfers between devices with their start and end apart: 4, of which 2 were waited for; matrix products, arithmetic and copies ran while one was open for 1% of the time, Pallas kernels for 0%

profile of v3, /device:TPU:0, one launch (start us, length us, event | category | flops | bytes accessed | tf_op | source)
XLA Modules:
  0.0 124.8 jit_solution(14941796469685370929)
XLA Ops:
  0.7 0.1 pad_add_fusion.1
  0.8 0.8 fusion.1
  1.6 1.0 slice_bitcast_fusion.5
  2.6 2.0 %fusion.3 = (bf16[4,64,1,256]{3,2,1,0:T(2,128)(2,1)S(1)}, bf16[4,64,1,256]{3,2,1,0:T(2,128)(2,1)S(1)}) fusion(bf16[4,64,64,256]{3,2,1,0:T(8,128)(2,1)} %x_ref.1), kind=kLoop, calls=%fused_computation.23 | loop fusion | bytes 524288 | tf_op jit(solution)/shard_map/slice | solution.py:547
  4.7 0.1 pad_maximum_fusion
  4.7 0.6 gather_fusion
  5.3 0.1 broadcast_select_fusion
  5.5 3.0 %collective-permute-start = (bf16[4,64,256]{2,1,0:T(8,128)(2,1)S(1)}, bf16[4,64,256]{2,1,0:T(8,128)(2,1)S(1)}, u32[]{:S(2)}, u32[]{:S(2)}) collective-permute-start(bf16[4,64,256]{2,1,0:T(8,128)(2,1)S(1)} %get-tuple-element.24), channel_id=1, source_target_pairs={{0,8},{8,16},{16,24},{24,0},{1,9},{9,17},{17,25},{25,1},{2,10},{10... | collective-permute-start | bytes 393224 | tf_op jit(solution)/shard_map/ppermute | solution.py:247
  8.5 0.0 collective-permute-start.3
  8.5 1.1 collective-permute-start.2
  9.6 3.2 %collective-permute-start.1 = (bf16[4,64,256]{2,1,0:T(8,128)(2,1)S(1)}, bf16[4,64,256]{2,1,0:T(8,128)(2,1)S(1)}, u32[]{:S(2)}, u32[]{:S(2)}) collective-permute-start(bf16[4,64,256]{2,1,0:T(8,128)(2,1)S(1)} %get-tuple-element.27), channel_id=1, source_target_pairs={{1,0},{2,1},{3,2},{4,3},{5,4},{6,5},{7,6},{0,7},{9,8},{10,9},{11,1... | collective-permute-start | bytes 393224 | tf_op jit(solution)/shard_map/ppermute | solution.py:248
  12.8 0.7 pad_add_fusion.links_ref
  13.5 0.0 collective-permute-done
  13.5 1.2 collective-permute-done.3
  14.7 1.3 %collective-permute-done.2 = bf16[4,64,256]{2,1,0:T(8,128)(2,1)S(1)} collective-permute-done((bf16[4,64,256]{2,1,0:T(8,128)(2,1)S(1)}, bf16[4,64,256]{2,1,0:T(8,128)(2,1)S(1)}, u32[]{:S(2)}, u32[]{:S(2)}) %collective-permute-start.2) | collective-permute-done | bytes 131104 | tf_op jit(solution)/shard_map/ppermute | solution.py:249
  16.0 0.0 collective-permute-done.1
  16.0 0.1 pad_maximum_fusion.1.rims_ref
  16.1 0.0 copy-start
  16.1 0.9 copy-done
  17.0 0.0 copy-start.1
  17.0 0.7 copy-done.1
  17.7 0.0 copy-start.3
  17.7 0.7 copy-done.3
  18.4 0.0 copy-start.2
  18.4 61.0 %shard_map.111 = (bf16[4,64,64,256]{3,2,1,0:T(8,128)(2,1)}, bf16[4,4,64,256]{3,2,1,0:T(8,128)(2,1)S(1)}, f32[272,256]{1,0:T(8,128)S(1)}) custom-call(bf16[4,64,64,256]{3,2,1,0:T(8,128)(2,1)} %x_ref.1, bf16[4,64,64,256]{3,2,1,0:T(8,128)(2,1)} %cot_ref.1, bf16[4,4,64,256]{3,2,1,0:T(8,128)(2,1)S(1)} %pad_maximum_fusion.1.rims_ref, ...), custom_call_target="tpu_custom_call" | custom-call | flops 4294967296 | bytes 25165824 | tf_op jit(solution)/shard_map/pallas_call | solution.py:557
  79.4 24.6 %shard_map.112 = (bf16[4,256,256]{2,1,0:T(8,128)(2,1)S(1)}, f32[256,256]{1,0:T(8,128)S(1)}, f32[9,256]{1,0:T(8,128)S(1)}, f32[1,256]{1,0:T(1,128)S(1)}) custom-call(bf16[4,256,256]{2,1,0:T(8,128)(2,1)S(1)} %bitcast.36, f32[272,256]{1,0:T(8,128)S(1)} %get-tuple-element.13.sums_ref), custom_call_target="tpu_custom_call" | custom-call | tf_op jit(solution)/shard_map/pallas_call | solution.py:485
  104.0 0.0 copy-done.2
  104.1 18.8 %shard_map.113 = bf16[4,64,64,256]{3,2,1,0:T(8,128)(2,1)} custom-call(bf16[4,64,64,256]{3,2,1,0:T(8,128)(2,1)} %get-tuple-element.11.g_ref, bf16[4,4,64,256]{3,2,1,0:T(8,128)(2,1)S(1)} %bitcast.37, s32[3,4]{1,0:T(4,128)S(1)} %pad_add_fusion.links_ref, f32[9,256]{1,0:T(8,128)S(1)} %copy-done.2), custom_call_target="tpu_custom_call" | custom-call | flops 167772160 | bytes 16777216 | tf_op jit(solution)/shard_map/pallas_call | solution.py:608
  122.9 0.6 copy.26
  123.5 0.6 copy.27
  124.1 0.7 copy.28
  (5 shorter events, 0.1 us)
Async XLA Ops:
  5.5 8.0 %collective-permute-start = (bf16[4,64,256]{2,1,0:T(8,128)(2,1)S(1)}, bf16[4,64,256]{2,1,0:T(8,128)(2,1)S(1)}, u32[]{:S(2)}, u32[]{:S(2)}) collective-permute-start(bf16[4,64,256]{2,1,0:T(8,128)(2,1)S(1)} %get-tuple-element.24), channel_id=1, source_target_pairs={{0,8},{8,16},{16,24},{24,0},{1,9},{9,17},{17,25},{25,1},{2,10},{10... | collective-permute-start | bytes 393224 | tf_op jit(solution)/shard_map/ppermute | solution.py:247
  8.5 6.2 %collective-permute-start.3 = (bf16[4,64,256]{2,1,0:T(8,128)(2,1)S(1)}, bf16[4,64,256]{2,1,0:T(8,128)(2,1)S(1)}, u32[]{:S(2)}, u32[]{:S(2)}) collective-permute-start(bf16[4,64,256]{2,1,0:T(8,128)(2,1)S(1)} %get-tuple-element.25), channel_id=1, source_target_pairs={{0,1},{1,2},{2,3},{3,4},{4,5},{5,6},{6,7},{7,0},{8,9},{9,10},{10,1... | collective-permute-start | bytes 393224 | tf_op jit(solution)/shard_map/ppermute | solution.py:250
  8.5 7.5 %collective-permute-start.2 = (bf16[4,64,256]{2,1,0:T(8,128)(2,1)S(1)}, bf16[4,64,256]{2,1,0:T(8,128)(2,1)S(1)}, u32[]{:S(2)}, u32[]{:S(2)}) collective-permute-start(bf16[4,64,256]{2,1,0:T(8,128)(2,1)S(1)} %get-tuple-element.26), channel_id=1, source_target_pairs={{8,0},{16,8},{24,16},{0,24},{9,1},{17,9},{25,17},{1,25},{10,2},{18... | collective-permute-start | bytes 393224 | tf_op jit(solution)/shard_map/ppermute | solution.py:249
  9.6 6.4 %collective-permute-start.1 = (bf16[4,64,256]{2,1,0:T(8,128)(2,1)S(1)}, bf16[4,64,256]{2,1,0:T(8,128)(2,1)S(1)}, u32[]{:S(2)}, u32[]{:S(2)}) collective-permute-start(bf16[4,64,256]{2,1,0:T(8,128)(2,1)S(1)} %get-tuple-element.27), channel_id=1, source_target_pairs={{1,0},{2,1},{3,2},{4,3},{5,4},{6,5},{7,6},{0,7},{9,8},{10,9},{11,1... | collective-permute-start | bytes 393224 | tf_op jit(solution)/shard_map/ppermute | solution.py:248
  16.1 0.9 copy-start
  17.0 0.7 copy-start.1
  17.7 0.7 copy-start.3
  18.4 85.7 %copy-start.2 = (f32[9,256]{1,0:T(8,128)S(1)}, f32[9,256]{1,0:T(8,128)}, u32[]{:S(2)}) copy-start(f32[9,256]{1,0:T(8,128)} %taps_ref.3) | copy-start | bytes 27652
